TPU v7x, 32 devices: a whole 2x2x4 slice. The times are simulated.
32 devices in a mesh: dp: 8 (over z, x), tensor: 4 (over y, core).
Axes of the slice: x: 2, y: 2, z: 4, core: 2. Of those that a mesh axis runs over, the one named last changes fastest.
Arguments:
- block_input: bfloat16 [8192, 768], P(('dp', 'tensor')), may hold values from -6 to 6
- out_cotangent: bfloat16 [8192, 768], P(('dp', 'tensor')), may hold values from -6 to 6
- seq_lengths: int32 [8, 4], replicated, may hold values from 1 to 682, 1024 in all within a row
- pack_order: int32 [8], replicated, may hold values from 0 to 7, each once
- ln1_gain: float32 [768], replicated, may hold values from 0.5 to 1.5
- ln1_bias: float32 [768], replicated, may hold values from -1.5 to 1.5
- qkv_weight: float32 [768, 3, 768], P('dp', None, 'tensor'), may hold values from -0.21875 to 0.21875
- qv_bias: float32 [2, 768], P(None, 'tensor'), may hold values from -1.5 to 1.5
- attn_out_weight: float32 [768, 768], P('tensor', 'dp'), may hold values from -1.75 to 1.75
- attn_out_bias: float32 [768], replicated, may hold values from -1.5 to 1.5
- ln2_gain: float32 [768], replicated, may hold values from 0.5 to 1.5
- ln2_bias: float32 [768], replicated, may hold values from -1.5 to 1.5
- fc_weight: float32 [768, 3072], P('dp', 'tensor'), may hold values from -0.21875 to 0.21875
- fc_bias: float32 [3072], P('tensor'), may hold values from -1.5 to 1.5
- proj_weight: float32 [3072, 768], P('tensor', 'dp'), may hold values from -0.109375 to 0.109375
- proj_bias: float32 [768], replicated, may hold values from -1.5 to 1.5
Outputs:
- block_output: bfloat16 [8192, 768], P(('dp', 'tensor'))
- input_grad: bfloat16 [8192, 768], P(('dp', 'tensor'))
- ln1_gain_grad: float32 [768], replicated
- ln1_bias_grad: float32 [768], replicated
- qkv_weight_grad: float32 [768, 3, 768], P('dp', None, 'tensor')
- qv_bias_grad: float32 [2, 768], P(None, 'tensor')
- attn_out_weight_grad: float32 [768, 768], P('tensor', 'dp')
- attn_out_bias_grad: float32 [768], replicated
- ln2_gain_grad: float32 [768], replicated
- ln2_bias_grad: float32 [768], replicated
- fc_weight_grad: float32 [768, 3072], P('dp', 'tensor')
- fc_bias_grad: float32 [3072], P('tensor')
- proj_weight_grad: float32 [3072, 768], P('tensor', 'dp')
- proj_bias_grad: float32 [768], replicated
Inputs may be any that keep to these rules, and one draw needn't show every extreme that they name: `seq_lengths`: each row gives the lengths of the 4 sequences of one pack in order, sums to 1024, and its largest entry is 682. `pack_order`: a permutation of the 8 packs.
All inputs are finite; a program needn't handle non-finite values.
Results may differ from a plain program's by a relative error of at most 0.017.
Values may be sent and summed in bfloat16 or wider, within the bound.
A program may use at most 128 MiB of HBM per device.

v0:
```python
import jax
import jax.numpy as jnp
from jax import lax
from jax.sharding import PartitionSpec as P

HEAD_DIM = 64
EPSILON = 1e-05
MASKED = -1e30


def gelu_curve(values):
    return (
        0.5
        * values
        * (1.0 + jnp.tanh(0.7978845608028654 * (values + 0.044715 * values * values * values)))
    )


def contract(left_side, right_side, left_dim, right_dim):
    return lax.dot_general(
        left_side,
        right_side,
        (((left_dim,), (right_dim,)), ((), ())),
        preferred_element_type=jnp.float32,
    )


def normalize(rows_in, norm_gain, norm_bias):
    row_mean = jnp.mean(rows_in, axis=1, keepdims=True)
    row_var = jnp.mean(rows_in * rows_in, axis=1, keepdims=True) - row_mean * row_mean
    row_scale = lax.rsqrt(row_var + EPSILON)
    centered = (rows_in - row_mean) * row_scale
    return (centered, row_scale, (centered * norm_gain + norm_bias).astype(jnp.bfloat16))


def norm_back(grad_in, centered, row_scale, norm_gain):
    gain_grad = jnp.sum(grad_in * centered, axis=0)
    bias_grad = jnp.sum(grad_in, axis=0)
    scaled = grad_in * norm_gain
    back = row_scale * (
        scaled
        - jnp.mean(scaled, axis=1, keepdims=True)
        - centered * jnp.mean(scaled * centered, axis=1, keepdims=True)
    )
    return (back, gain_grad, bias_grad)


def grad_rows(local_rows):
    return lax.all_gather(local_rows, "tensor", axis=0, tiled=True)


def input_total(partial_value):
    return lax.psum_scatter(
        partial_value.astype(jnp.bfloat16), "tensor", scatter_dimension=0, tiled=True
    ).astype(jnp.float32)


def block_scores(query_rows, keys_seen, segment, begin_row):
    block_len = query_rows.shape[0]
    key_count = keys_seen.shape[0]
    row_pos = begin_row + jnp.arange(block_len, dtype=jnp.int32)
    col_pos = jnp.arange(key_count, dtype=jnp.int32)
    row_segment = segment[begin_row : begin_row + block_len]
    allowed = (col_pos[None, :] <= row_pos[:, None]) & (
        segment[None, :key_count] == row_segment[:, None]
    )
    raw_scores = jnp.einsum(
        "qhd,khd->hqk", query_rows, keys_seen, preferred_element_type=jnp.float32
    ) * query_rows.shape[2] ** (-0.5)
    return jnp.where(allowed[None], raw_scores, MASKED)


def attend(queries, keys_all, values_all, segment, block_len):
    outputs = []
    log_totals = []
    for begin_row in range(0, queries.shape[0], block_len):
        final_row = begin_row + block_len
        query_rows = queries[begin_row:final_row]
        scores = block_scores(query_rows, keys_all[:final_row], segment, begin_row)
        row_peak = jnp.max(scores, axis=-1, keepdims=True)
        weights = jnp.exp(scores - row_peak)
        weight_total = jnp.sum(weights, axis=-1, keepdims=True)
        probs = (weights / weight_total).astype(jnp.bfloat16)
        outputs.append(
            jnp.einsum(
                "hqk,khd->qhd", probs, values_all[:final_row], preferred_element_type=jnp.float32
            )
        )
        log_totals.append(row_peak + jnp.log(weight_total))
    return (jnp.concatenate(outputs, axis=0), log_totals)


def attend_back(queries, keys_all, values_all, segment, block_len, log_totals, out_grad):
    factor = queries.shape[2] ** (-0.5)
    key_grad = jnp.zeros(keys_all.shape, jnp.float32)
    value_grad = jnp.zeros(values_all.shape, jnp.float32)
    query_grads = []
    for block_index, begin_row in enumerate(range(0, queries.shape[0], block_len)):
        final_row = begin_row + block_len
        query_rows = queries[begin_row:final_row]
        keys_seen = keys_all[:final_row]
        values_seen = values_all[:final_row]
        grad_block = out_grad[begin_row:final_row]
        probs = jnp.exp(
            block_scores(query_rows, keys_seen, segment, begin_row) - log_totals[block_index]
        )
        value_grad = value_grad.at[:final_row].add(
            jnp.einsum(
                "hqk,qhd->khd",
                probs.astype(jnp.bfloat16),
                grad_block,
                preferred_element_type=jnp.float32,
            )
        )
        prob_grad = jnp.einsum(
            "qhd,khd->hqk", grad_block, values_seen, preferred_element_type=jnp.float32
        )
        row_delta = jnp.sum(probs * prob_grad, axis=-1, keepdims=True)
        score_grad = (probs * (prob_grad - row_delta)).astype(jnp.bfloat16)
        query_grads.append(
            jnp.einsum("hqk,khd->qhd", score_grad, keys_seen, preferred_element_type=jnp.float32)
            * factor
        )
        key_grad = key_grad.at[:final_row].add(
            jnp.einsum("hqk,qhd->khd", score_grad, query_rows, preferred_element_type=jnp.float32)
            * factor
        )
    return (jnp.concatenate(query_grads, axis=0), key_grad, value_grad)


def local(
    block_input,
    out_cotangent,
    seq_lengths,
    pack_order,
    ln1_gain,
    ln1_bias,
    qkv_weight,
    qv_bias,
    attn_out_weight,
    attn_out_bias,
    ln2_gain,
    ln2_bias,
    fc_weight,
    fc_bias,
    proj_weight,
    proj_bias,
):
    local_rows, width = block_input.shape
    pack_count = pack_order.shape[0]
    piece_rows = local_rows // pack_count
    pack_rows = local_rows * lax.axis_size("tensor")
    head_cols = qv_bias.shape[1]
    heads_here = head_cols // HEAD_DIM
    block_len = min(512, pack_rows)
    slots = jnp.arange(pack_count, dtype=jnp.int32)
    inverse = jnp.sum(jnp.where(pack_order[None, :] == slots[:, None], slots[None, :], 0), axis=1)
    sent_input = jnp.take(
        block_input.reshape(pack_count, piece_rows, width), inverse, axis=0
    ).reshape(local_rows, width)
    sent_grad = jnp.take(
        out_cotangent.reshape(pack_count, piece_rows, width), inverse, axis=0
    ).reshape(local_rows, width)
    arrived = (
        lax.all_to_all(sent_input, "dp", split_axis=0, concat_axis=0, tiled=True),
        lax.all_to_all(sent_grad, "dp", split_axis=0, concat_axis=0, tiled=True),
    )
    input_here = arrived[0].astype(jnp.float32)
    grad_here = arrived[1].astype(jnp.float32)
    my_pack = lax.axis_index("dp")
    my_lengths = lax.dynamic_index_in_dim(seq_lengths, my_pack, 0, keepdims=False)
    seq_ends = jnp.cumsum(my_lengths)
    positions = jnp.arange(pack_rows, dtype=jnp.int32)
    segment = jnp.sum((positions[:, None] >= seq_ends[None, :]).astype(jnp.int32), axis=1)
    weights = (
        lax.all_gather(qkv_weight.astype(jnp.bfloat16), "dp", axis=0, tiled=True),
        lax.all_gather(attn_out_weight.astype(jnp.bfloat16), "dp", axis=1, tiled=True),
        lax.all_gather(fc_weight.astype(jnp.bfloat16), "dp", axis=0, tiled=True),
        lax.all_gather(proj_weight.astype(jnp.bfloat16), "dp", axis=1, tiled=True),
    )
    qkv_full = weights[0].reshape(width, 3 * head_cols)
    out_full = weights[1]
    fc_full = weights[2]
    proj_full = weights[3]
    centered_one, scale_one, ln_one = normalize(input_here, ln1_gain, ln1_bias)
    normed_one = lax.all_gather(ln_one, "tensor", axis=0, tiled=True)
    projected = jnp.dot(normed_one, qkv_full, preferred_element_type=jnp.float32)
    queries = (
        (projected[:, :head_cols] + qv_bias[0])
        .astype(jnp.bfloat16)
        .reshape(pack_rows, heads_here, HEAD_DIM)
    )
    keys_all = (
        projected[:, head_cols : 2 * head_cols]
        .astype(jnp.bfloat16)
        .reshape(pack_rows, heads_here, HEAD_DIM)
    )
    values_all = (
        (projected[:, 2 * head_cols :] + qv_bias[1])
        .astype(jnp.bfloat16)
        .reshape(pack_rows, heads_here, HEAD_DIM)
    )
    attended, log_totals = attend(queries, keys_all, values_all, segment, block_len)
    attended_low = attended.reshape(pack_rows, head_cols).astype(jnp.bfloat16)
    attn_partial = jnp.dot(attended_low, out_full, preferred_element_type=jnp.float32)
    attn_here = lax.psum_scatter(
        attn_partial.astype(jnp.bfloat16), "tensor", scatter_dimension=0, tiled=True
    ).astype(jnp.float32)
    resid_one = input_here + attn_here + attn_out_bias
    centered_two, scale_two, ln_two = normalize(resid_one, ln2_gain, ln2_bias)
    normed_two = lax.all_gather(ln_two, "tensor", axis=0, tiled=True)
    upper_pre = jnp.dot(normed_two, fc_full, preferred_element_type=jnp.float32) + fc_bias
    activated = gelu_curve(upper_pre).astype(jnp.bfloat16)
    mlp_here = lax.psum_scatter(
        jnp.dot(activated, proj_full, preferred_element_type=jnp.float32).astype(jnp.bfloat16),
        "tensor",
        scatter_dimension=0,
        tiled=True,
    ).astype(jnp.float32)
    block_output = (resid_one + mlp_here + proj_bias).astype(jnp.bfloat16)
    proj_bias_grad = jnp.sum(grad_here, axis=0)
    mlp_grad = grad_rows(grad_here.astype(jnp.bfloat16))
    proj_grad = contract(activated, mlp_grad, 0, 0)
    act_grad = contract(mlp_grad, proj_full, 1, 1)
    gelu_pull = jax.vjp(gelu_curve, upper_pre)[1]
    upper_grad = gelu_pull(act_grad)[0].astype(jnp.bfloat16)
    fc_bias_grad = jnp.sum(upper_grad.astype(jnp.float32), axis=0)
    fc_grad = contract(normed_two, upper_grad, 0, 0)
    normed_two_grad = input_total(contract(upper_grad, fc_full, 1, 1))
    back_two, ln2_gain_grad, ln2_bias_grad = norm_back(
        normed_two_grad, centered_two, scale_two, ln2_gain
    )
    resid_grad = grad_here + back_two
    attn_out_bias_grad = jnp.sum(resid_grad, axis=0)
    attn_grad_rows = grad_rows(resid_grad.astype(jnp.bfloat16))
    out_weight_grad = contract(attended_low, attn_grad_rows, 0, 0)
    attended_grad = (
        contract(attn_grad_rows, out_full, 1, 1)
        .astype(jnp.bfloat16)
        .reshape(pack_rows, heads_here, HEAD_DIM)
    )
    query_grad, key_grad, value_grad = attend_back(
        queries, keys_all, values_all, segment, block_len, log_totals, attended_grad
    )
    query_low = query_grad.reshape(pack_rows, head_cols).astype(jnp.bfloat16)
    key_low = key_grad.reshape(pack_rows, head_cols).astype(jnp.bfloat16)
    value_low = value_grad.reshape(pack_rows, head_cols).astype(jnp.bfloat16)
    qv_bias_grad = jnp.stack(
        [
            jnp.sum(query_low.astype(jnp.float32), axis=0),
            jnp.sum(value_low.astype(jnp.float32), axis=0),
        ]
    )
    joined_grad = jnp.concatenate([query_low, key_low, value_low], axis=1)
    qkv_grad = contract(normed_one, joined_grad, 0, 0).reshape(width, 3, head_cols)
    normed_one_grad = input_total(contract(joined_grad, qkv_full, 1, 1))
    back_one, ln1_gain_grad, ln1_bias_grad = norm_back(
        normed_one_grad, centered_one, scale_one, ln1_gain
    )
    input_grad = (resid_grad + back_one).astype(jnp.bfloat16)
    returned = (
        lax.all_to_all(block_output, "dp", split_axis=0, concat_axis=0, tiled=True),
        lax.all_to_all(input_grad, "dp", split_axis=0, concat_axis=0, tiled=True),
    )
    out_rows = jnp.take(
        returned[0].reshape(pack_count, piece_rows, width), pack_order, axis=0
    ).reshape(local_rows, width)
    grad_out_rows = jnp.take(
        returned[1].reshape(pack_count, piece_rows, width), pack_order, axis=0
    ).reshape(local_rows, width)
    all_sums = (
        lax.psum_scatter(qkv_grad, "dp", scatter_dimension=0, tiled=True),
        lax.psum_scatter(out_weight_grad, "dp", scatter_dimension=1, tiled=True),
        lax.psum_scatter(fc_grad, "dp", scatter_dimension=0, tiled=True),
        lax.psum_scatter(proj_grad, "dp", scatter_dimension=1, tiled=True),
    )
    qkv_sum, out_sum, fc_sum, proj_sum = (all_sums[0], all_sums[1], all_sums[2], all_sums[3])
    head_sums = lax.psum((qv_bias_grad, fc_bias_grad), "dp")
    shared_sums = lax.psum(
        (
            ln1_gain_grad,
            ln1_bias_grad,
            attn_out_bias_grad,
            ln2_gain_grad,
            ln2_bias_grad,
            proj_bias_grad,
        ),
        ("dp", "tensor"),
    )
    return (
        out_rows,
        grad_out_rows,
        shared_sums[0],
        shared_sums[1],
        qkv_sum,
        head_sums[0],
        out_sum,
        shared_sums[2],
        shared_sums[3],
        shared_sums[4],
        fc_sum,
        head_sums[1],
        proj_sum,
        shared_sums[5],
    )


def solution(mesh):
    return jax.shard_map(
        local,
        mesh=mesh,
        in_specs=(
            P(("dp", "tensor"), None),
            P(("dp", "tensor"), None),
            P(),
            P(),
            P(),
            P(),
            P("dp", None, "tensor"),
            P(None, "tensor"),
            P("tensor", "dp"),
            P(),
            P(),
            P(),
            P("dp", "tensor"),
            P("tensor"),
            P("tensor", "dp"),
            P(),
        ),
        out_specs=(
            P(("dp", "tensor"), None),
            P(("dp", "tensor"), None),
            P(),
            P(),
            P("dp", None, "tensor"),
            P(None, "tensor"),
            P("tensor", "dp"),
            P(),
            P(),
            P(),
            P("dp", "tensor"),
            P("tensor"),
            P("tensor", "dp"),
            P(),
        ),
        check_vma=False,
    )
```

profile of v0, /device:TPU:0, one launch (start us, length us, event | category | flops | bytes accessed | tf_op | source)
XLA Modules:
  0.0 679.9 jit_solution(4538594426250467787)
XLA Ops:
  12.1 19.1 %all_to_all.33 = bf16[8,32,768]{2,1,0:T(8,128)(2,1)S(1)} all-to-all(bf16[8,32,768]{2,1,0:T(8,128)(2,1)S(1)} %get-tuple-element.121), channel_id=1, replica_groups=mesh['dp'=8,'tensor'=4] {'dp'}, dimensions={0} | all-to-all | bytes 786432 | tf_op jit(solution)/shard_map/all_to_all | solution.py:165
  33.3 36.0 %all_gather.25 = bf16[768,3,192]{2,1,0:T(4,128)(2,1)S(1)} all-gather(bf16[96,3,192]{2,1,0:T(4,128)(2,1)S(1)} %copy.57), channel_id=1, replica_groups=mesh['dp'=8,'tensor'=4] {'dp'}, dimensions={0}, use_global_device_ids=true | all-gather | bytes 995328 | tf_op jit(solution)/shard_map/all_gather | solution.py:176
  70.3 33.0 %all_gather.26 = bf16[192,768]{0,1:T(8,128)(2,1)} all-gather(bf16[192,96]{0,1:T(8,128)(2,1)S(1)} %copy.60), channel_id=1, replica_groups=mesh['dp'=8,'tensor'=4] {'dp'}, dimensions={1}, use_global_device_ids=true | all-gather | bytes 331776 | tf_op jit(solution)/shard_map/all_gather | solution.py:177
  105.5 2.5 fusion.80
  121.6 25.3 %reduce-scatter.11.cloned.1.call-done = bf16[256,768]{1,0:T(8,128)(2,1)} async-done(((bf16[1024,768]{1,0:T(8,128)(2,1)}), bf16[256,768]{1,0:T(8,128)(2,1)}) %reduce-scatter.11.cloned.1.call-update) | async-done | bytes 393232 | tf_op jit(solution)/shard_map/reduce_scatter | solution.py:206
  152.6 18.5 %all_to_all.34 = bf16[8,32,768]{2,1,0:T(8,128)(2,1)} all-to-all(bf16[8,32,768]{2,1,0:T(8,128)(2,1)} %get-tuple-element.120), channel_id=1, replica_groups=mesh['dp'=8,'tensor'=4] {'dp'}, dimensions={0} | all-to-all | bytes 786432 | tf_op jit(solution)/shard_map/all_to_all | solution.py:166
  171.4 14.1 %all-gather.9.cloned.1.call-done = bf16[1024,768]{1,0:T(8,128)(2,1)} async-done(((bf16[256,768]{1,0:T(8,128)(2,1)}), bf16[1024,768]{1,0:T(8,128)(2,1)}) %all-gather.9.cloned.1.call-update) | async-done | bytes 1572880 | tf_op jit(solution)/shard_map/all_gather | solution.py:211
  185.5 4.9 fusion.83
  190.4 39.0 %all-gather.13.cloned.1.call-done = bf16[768,768]{0,1:T(8,128)(2,1)} async-done(((bf16[768,96]{0,1:T(8,128)(2,1)}), bf16[768,768]{0,1:T(8,128)(2,1)}) %all-gather.13.cloned.1.call-update) | async-done | bytes 1179664 | tf_op jit(solution)/shard_map/all_gather | solution.py:179
  229.3 19.7 %all-gather.15.cloned.1.call-done = bf16[1024,768]{1,0:T(8,128)(2,1)} async-done(((bf16[256,768]{1,0:T(8,128)(2,1)}), bf16[1024,768]{1,0:T(8,128)(2,1)}) %all-gather.15.cloned.1.call-update) | async-done | bytes 1572880 | tf_op jit(solution)/shard_map/all_gather | solution.py:49
  249.0 6.9 %convert_reduce_fusion = (f32[768]{0:T(1024)}, bf16[1024,768]{1,0:T(8,128)(2,1)S(1)}) fusion(f32[1024,768]{1,0:T(8,128)} %fusion.83, f32[768]{0:T(1024)} %param.43, bf16[1024,768]{1,0:T(8,128)(2,1)} %all-gather.15.cloned.1.call-done, bf16[768,768]{0,1:T(8,128)(2,1)} %all-gather.13.cloned.1.call-done), kind=kOutput, calls=%fused_computation.23 | convolution fusion | flops 1229192448 | bytes 7477248 | tf_op jit(solution)/shard_map/dot_general | solution.py:20
  257.1 2.6 convolution_convert_fusion.1
  259.7 5.5 convolution_convert_fusion.2
  265.3 22.7 %reduce-scatter.15.cloned.1.call-done = bf16[256,768]{1,0:T(8,128)(2,1)} async-done(((bf16[1024,768]{1,0:T(8,128)(2,1)}), bf16[256,768]{1,0:T(8,128)(2,1)}) %reduce-scatter.15.cloned.1.call-update) | async-done | bytes 393232 | tf_op jit(solution)/shard_map/reduce_scatter | solution.py:53
  291.4 27.2 %reduce-scatter.13.cloned.1.call-done = bf16[256,768]{1,0:T(8,128)(2,1)} async-done(((bf16[1024,768]{1,0:T(8,128)(2,1)}), bf16[256,768]{1,0:T(8,128)(2,1)}) %reduce-scatter.13.cloned.1.call-update) | async-done | bytes 393232 | tf_op jit(solution)/shard_map/reduce_scatter | solution.py:214
  318.6 3.3 fusion.74
  325.3 17.9 %all-gather.17.cloned.1.call-done = bf16[1024,768]{1,0:T(8,128)(2,1)} async-done(((bf16[256,768]{1,0:T(8,128)(2,1)}), bf16[1024,768]{1,0:T(8,128)(2,1)}) %all-gather.17.cloned.1.call-update) | async-done | bytes 1572880 | tf_op jit(solution)/shard_map/all_gather | solution.py:49
  357.4 2.6 convolution_convert_fusion
  361.7 5.6 fusion.72
  367.7 5.1 fusion.84
  373.0 2.4 fusion.68
  375.4 3.1 copy.64
  378.5 5.7 all-to-all-start.1
  384.2 4.0 reduce-scatter.17.cloned.1.call-done
  391.8 4.5 all-to-all-done.1
  396.3 3.6 all-to-all-start.3
  400.8 23.4 %all-reduce.3 = (f32[2,192]{1,0:T(2,128)}, f32[768]{0:T(1024)}) all-reduce(f32[2,192]{1,0:T(2,128)S(1)} %pad_maximum_fusion.4, f32[768]{0:T(1024)S(1)} %copy-done.52), channel_id=1, replica_groups=mesh['dp'=8,'tensor'=4] {'dp'}, use_global_device_ids=true, to_apply=%region_28.30 | all-reduce | flops 1152 | bytes 9216 | tf_op jit(solution)/shard_map/psum | solution.py:278
  424.3 30.8 %reduce-scatter.25.cloned.1.call-done = f32[96,192]{1,0:T(8,128)} async-done(((f32[768,192]{1,0:T(8,128)}), f32[96,192]{1,0:T(8,128)}) %reduce-scatter.25.cloned.1.call-update) | async-done | bytes 73744
  456.7 41.3 %all-reduce.2 = (f32[768]{0:T(1024)}, f32[768]{0:T(1024)}, f32[768]{0:T(1024)}, f32[768]{0:T(1024)}, f32[768]{0:T(1024)}, /*index=5*/f32[768]{0:T(1024)}) all-reduce(f32[768]{0:T(1024)S(1)} %get-tuple-element.83, f32[768]{0:T(1024)S(1)} %get-tuple-element.88, ...), channel_id=1, replica_groups=mesh['dp'=8,'tensor'=4] {'dp','tensor'}, use_global_device_ids=true, to_apply=%region_22.24 | all-reduce | flops 4608 | bytes 36864 | tf_op jit(solution)/shard_map/psum | solution.py:279
  499.6 28.4 %reduce-scatter.23.cloned.1.call-done = f32[768,96]{0,1:T(8,128)} async-done(((f32[768,768]{0,1:T(8,128)}), f32[768,96]{0,1:T(8,128)}) %reduce-scatter.23.cloned.1.call-update) | async-done | bytes 294928 | tf_op jit(solution)/shard_map/reduce_scatter | solution.py:275
  527.9 72.4 %reduce-scatter.21.cloned.1.call-done = f32[96,768]{1,0:T(8,128)} async-done(((f32[768,768]{1,0:T(8,128)}), f32[96,768]{1,0:T(8,128)}) %reduce-scatter.21.cloned.1.call-update) | async-done | bytes 294928 | tf_op jit(solution)/shard_map/reduce_scatter | solution.py:274
  600.3 72.5 %reduce-scatter.19.cloned.1.call-done = f32[96,3,192]{2,0,1:T(8,128)} async-done(((f32[768,3,192]{2,0,1:T(8,128)}), f32[96,3,192]{2,0,1:T(8,128)}) %reduce-scatter.19.cloned.1.call-update) | async-done | bytes 221200 | tf_op jit(solution)/shard_map/reduce_scatter | solution.py:272
  (232 shorter events, 60.3 us)
Async XLA Ops:
  8.0 23.6 %copy-start.38 = (f32[768]{0:T(1024)S(1)}, f32[768]{0:T(1024)}, u32[]{:S(2)}) copy-start(f32[768]{0:T(1024)} %param.34) | copy-start | bytes 9220
  8.0 23.6 %copy-start.51 = (f32[768]{0:T(1024)S(1)}, f32[768]{0:T(1024)}, u32[]{:S(2)}) copy-start(f32[768]{0:T(1024)} %param.35) | copy-start | bytes 9220
  8.1 24.6 %copy-start.53 = (s32[8,4]{0,1:T(4,128)S(1)}, s32[8,4]{0,1:T(4,128)}, u32[]{:S(2)}) copy-start(s32[8,4]{0,1:T(4,128)} %param.32) | copy-start | bytes 388
  8.1 25.0 %copy-start.34 = (f32[192,96]{1,0:T(8,128)S(1)}, f32[192,96]{1,0:T(8,128)}, u32[]{:S(2)}) copy-start(f32[192,96]{1,0:T(8,128)} %param.38) | copy-start | bytes 221188
  8.1 25.1 %copy-start.33 = (f32[96,3,192]{2,0,1:T(8,128)S(1)}, f32[96,3,192]{2,0,1:T(8,128)}, u32[]{:S(2)}) copy-start(f32[96,3,192]{2,0,1:T(8,128)} %param.36) | copy-start | bytes 663556
  8.1 97.5 %all-gather.7.cloned.1.call-start = ((), (), s32[]{:S(2)}) async-start(), calls=%async_computation.12 | async-start | bytes 1966080 | tf_op jit(solution)/shard_map/all_gather | solution.py:186
  31.5 38.7 %copy-start.42 = (f32[256]{0:T(256)}, f32[256]{0:T(256)S(1)}, u32[]{:S(2)}) copy-start(f32[256]{0:T(256)S(1)} %div.45) | copy-start | bytes 3076
  31.6 38.6 %copy-start.44 = (f32[256]{0:T(256)}, f32[256]{0:T(256)S(1)}, u32[]{:S(2)}) copy-start(f32[256]{0:T(256)S(1)} %add_rsqrt_fusion.1) | copy-start | bytes 3076
  32.6 70.7 %copy-start.54 = (f32[2,192]{1,0:T(2,128)S(1)}, f32[2,192]{1,0:T(2,128)}, u32[]{:S(2)}) copy-start(f32[2,192]{1,0:T(2,128)} %param.37) | copy-start | bytes 4612
  32.6 114.3 %reduce-scatter.11.cloned.1.call-start = ((), (), s32[]{:S(2)}) async-start(), calls=%async_computation.13 | async-start | bytes 1966080 | tf_op jit(solution)/shard_map/reduce_scatter | solution.py:206
  70.2 37.9 %copy-start.9 = (bf16[768,3,192]{0,2,1:T(8,128)(2,1)}, bf16[768,3,192]{0,2,1:T(8,128)(2,1)S(1)}, u32[]{:S(2)}) copy-start(bf16[768,3,192]{0,2,1:T(8,128)(2,1)S(1)} %copy.58) | copy-start | bytes 2654212
  117.2 29.7 %copy-start.36 = (f32[768]{0:T(1024)S(1)}, f32[768]{0:T(1024)}, u32[]{:S(2)}) copy-start(f32[768]{0:T(1024)} %param.39) | copy-start | bytes 9220
  117.2 31.6 %copy-start.37 = (f32[768]{0:T(1024)S(1)}, f32[768]{0:T(1024)}, u32[]{:S(2)}) copy-start(f32[768]{0:T(1024)} %param.40) | copy-start | bytes 9220
  119.8 51.5 %all-gather.11.cloned.1.call-start = ((), (), s32[]{:S(2)}) async-start(), calls=%async_computation.15 | async-start | bytes 1327104 | tf_op jit(solution)/shard_map/all_gather | solution.py:178
  121.6 63.9 %all-gather.9.cloned.1.call-start = ((), (), s32[]{:S(2)}) async-start(), calls=%async_computation.14 | async-start | bytes 1966080 | tf_op jit(solution)/shard_map/all_gather | solution.py:211
  150.8 78.5 %all-gather.13.cloned.1.call-start = ((), (), s32[]{:S(2)}) async-start(), calls=%async_computation.16 | async-start | bytes 1327104 | tf_op jit(solution)/shard_map/all_gather | solution.py:179
  152.5 96.5 %all-gather.15.cloned.1.call-start = ((), (), s32[]{:S(2)}) async-start(), calls=%async_computation.18 | async-start | bytes 1966080 | tf_op jit(solution)/shard_map/all_gather | solution.py:49
  171.1 116.9 %reduce-scatter.15.cloned.1.call-start = ((), (), s32[]{:S(2)}) async-start(), calls=%async_computation.19 | async-start | bytes 1966080 | tf_op jit(solution)/shard_map/reduce_scatter | solution.py:53
  259.7 58.9 %reduce-scatter.13.cloned.1.call-start = ((), (), s32[]{:S(2)}) async-start(), calls=%async_computation.17 | async-start | bytes 1966080 | tf_op jit(solution)/shard_map/reduce_scatter | solution.py:214
  265.3 77.9 %all-gather.17.cloned.1.call-start = ((), (), s32[]{:S(2)}) async-start(), calls=%async_computation.20 | async-start | bytes 1966080 | tf_op jit(solution)/shard_map/all_gather | solution.py:49
  323.6 64.6 %reduce-scatter.17.cloned.1.call-start = ((), (), s32[]{:S(2)}) async-start(), calls=%async_computation.21 | async-start | bytes 1966080 | tf_op jit(solution)/shard_map/reduce_scatter | solution.py:53
  360.0 95.1 %reduce-scatter.25.cloned.1.call-start = ((), (), s32[]{:S(2)}) async-start(), calls=%async_computation.25 | async-start | bytes 884736
  361.7 166.3 %reduce-scatter.23.cloned.1.call-start = ((), (), s32[]{:S(2)}) async-start(), calls=%async_computation.24 | async-start | bytes 2654208 | tf_op jit(solution)/shard_map/reduce_scatter | solution.py:275
  367.4 232.9 %reduce-scatter.21.cloned.1.call-start = ((), (), s32[]{:S(2)}) async-start(), calls=%async_computation.23 | async-start | bytes 2654208 | tf_op jit(solution)/shard_map/reduce_scatter | solution.py:274
  372.9 299.9 %reduce-scatter.19.cloned.1.call-start = ((), (), s32[]{:S(2)}) async-start(), calls=%async_computation.22 | async-start | bytes 2654208 | tf_op jit(solution)/shard_map/reduce_scatter | solution.py:272
  378.5 22.4 %copy-start.52 = (f32[768]{0:T(1024)S(1)}, f32[768]{0:T(1024)}, u32[]{:S(2)}) copy-start(f32[768]{0:T(1024)} %get-tuple-element.99) | copy-start | bytes 9220
  378.5 78.2 %copy-start.48 = (f32[768]{0:T(1024)S(1)}, f32[768]{0:T(1024)}, u32[]{:S(2)}) copy-start(f32[768]{0:T(1024)} %get-tuple-element.79) | copy-start | bytes 9220
  378.5 78.2 %copy-start.49 = (f32[768]{0:T(1024)S(1)}, f32[768]{0:T(1024)}, u32[]{:S(2)}) copy-start(f32[768]{0:T(1024)} %get-tuple-element.87) | copy-start | bytes 9220
  378.5 78.2 %copy-start.50 = (f32[768]{0:T(1024)S(1)}, f32[768]{0:T(1024)}, u32[]{:S(2)}) copy-start(f32[768]{0:T(1024)} %get-tuple-element.103) | copy-start | bytes 9220
  378.5 17.8 %all-to-all-start.1 = ((bf16[8,32,768]{2,1,0:T(8,128)(2,1)}), bf16[8,32,768]{2,1,0:T(8,128)(2,1)S(1)}, u32[]{:S(2)}, u32[]{:S(2)}) async-start(bf16[8,32,768]{2,1,0:T(8,128)(2,1)} %bitcast.15), calls=%async_computation.3 | async-start | bytes 786432 | tf_op jit(solution)/shard_map/all_to_all | solution.py:262
  389.6 283.2 %copy-start.1 = (bf16[256,768]{1,0:T(8,128)(2,1)S(1)}, bf16[256,768]{1,0:T(8,128)(2,1)}, u32[]{:S(2)}) copy-start(bf16[256,768]{1,0:T(8,128)(2,1)} %param.31) | copy-start | bytes 1179652
  396.3 101.7 %all-to-all-start.3 = ((bf16[8,32,768]{2,1,0:T(8,128)(2,1)}), bf16[8,32,768]{2,1,0:T(8,128)(2,1)S(1)}, u32[]{:S(2)}, u32[]{:S(2)}) async-start(bf16[8,32,768]{2,1,0:T(8,128)(2,1)} %bitcast.30), calls=%async_computation.7 | async-start | bytes 786432 | tf_op jit(solution)/shard_map/all_to_all | solution.py:263
  (45 other events, 189.8 us)
Sparse Core Ops, SparseCore 0:
  32.8 18.3 all-gather.6
  120.0 26.9 reduce-scatter.10
  259.8 28.1 reduce-scatter.14
  290.4 28.1 reduce-scatter.12
Sparse Core Ops, SparseCore 1:
  123.3 41.1 all-gather.10
  166.5 18.9 all-gather.8
  187.8 41.5 all-gather.12
  231.0 18.0 all-gather.14
  323.7 19.5 all-gather.16
  360.0 28.1 reduce-scatter.16
  391.3 63.7 reduce-scatter.24
  459.4 68.5 reduce-scatter.22
  532.3 68.0 reduce-scatter.20
  604.8 67.9 reduce-scatter.18
where the time goes:
time: 681 us; the launch traced here: 680 us
  waiting for transfers between devices  379 us (56%)
  blocking collectives  171 us (25%)
  matrix products  55.5 us (8%)
  other arithmetic  30.1 us (4%)
  local copies, waits for them, and re-layouts  17.6 us (3%)
  between operations  16.2 us (2%)
  starting transfers between devices  10.6 us (2%)
    reduce_scatter x1, waiting for transfers between devices, local(): lax.psum_scatter(qkv_grad, 'dp', scatter_dimension=0, tiled=True)  72.5 us
    reduce_scatter x1, waiting for transfers between devices, local(): lax.psum_scatter(fc_grad, 'dp', scatter_dimension=0, tiled=True)  72.4 us
    psum x1, blocking collectives, local(): lax.psum((ln1_gain_grad, ln1_bias_grad, attn_out_bias_grad, ln2_gain_grad...  41.3 us
    all_gather x1, waiting for transfers between devices, local(): lax.all_gather(proj_weight.astype(jnp.bfloat16), 'dp', axis=1, tiled=True)  39 us
    all_gather x2, waiting for transfers between devices, grad_rows(): return lax.all_gather(local_rows, 'tensor', axis=0, tiled=True)  37.6 us
    all_gather x1, blocking collectives, local(): lax.all_gather(qkv_weight.astype(jnp.bfloat16), 'dp', axis=0, tiled=True)  36 us
    all_gather x1, blocking collectives, local(): lax.all_gather(attn_out_weight.astype(jnp.bfloat16), 'dp', axis=1, tiled=...  33 us
    unnamed x15, waiting for transfers between devices  31 us
  transfers between devices with their start and end apart: 16, of which 13 were waited for; matrix products, arithmetic and copies ran while one was open for 7% of the time, Pallas kernels for 0%

commit v1 on v0

--- a/solution.py
+++ b/solution.py
@@ -6,6 +6,18 @@
 HEAD_DIM = 64
 EPSILON = 1e-05
 MASKED = -1e30
+
+
+def rotated_exchange(shard, axis, split, join):
+    ways, here = (lax.axis_size(axis), lax.axis_index(axis))
+    width = shard.shape[split] // ways
+    turned = jnp.roll(shard, -here * width, axis=split)
+    got = [lax.slice_in_dim(turned, 0, width, axis=split)]
+    for far in range(1, ways):
+        sent = lax.slice_in_dim(turned, far * width, (far + 1) * width, axis=split)
+        got.append(lax.ppermute(sent, axis, [(d, (d + far) % ways) for d in range(ways)]))
+    line = jnp.concatenate(got[::-1], axis=join)
+    return jnp.roll(line, (here + 1) * got[0].shape[join], axis=join)
 
 
 def gelu_curve(values):
@@ -162,7 +174,7 @@
         out_cotangent.reshape(pack_count, piece_rows, width), inverse, axis=0
     ).reshape(local_rows, width)
     arrived = (
-        lax.all_to_all(sent_input, "dp", split_axis=0, concat_axis=0, tiled=True),
+        rotated_exchange(sent_input, "dp", 0, 0),
         lax.all_to_all(sent_grad, "dp", split_axis=0, concat_axis=0, tiled=True),
     )
     input_here = arrived[0].astype(jnp.float32)

time: 681 us -> 695 us (1.021); the launches traced: 680 us -> 686 us
  starting transfers between devices: 10.6 us -> 26.8 us
  blocking collectives: 171 us -> 155 us
    all_to_all x1 -> x0, blocking collectives: 19.1 us -> none  [local(): lax.all_to_all(sent_input, 'dp', split_axis=0, concat_axis=0, tiled=True)]
    ppermute x0 -> x7, starting transfers between devices: none -> 16 us  [rotated_exchange(): lax.ppermute(sent, axis, [(d, (d + far) % ways) for d in range(ways)])]
  transfers between devices with their start and end apart: 16 -> 23, of which waited for: 13 -> 15; matrix products, arithmetic and copies ran while one was open for 7% -> 7% of each run, Pallas kernels for 0% -> 0%
where the time goes in v1:
time: 695 us; the launch traced here: 686 us
  waiting for transfers between devices  384 us (55%)
  blocking collectives  155 us (22%)
  matrix products  55.5 us (8%)
  other arithmetic  30.6 us (4%)
  starting transfers between devices  26.8 us (4%)
  local copies, waits for them, and re-layouts  17.5 us (3%)
  between operations  16.6 us (2%)
    reduce_scatter x1, waiting for transfers between devices, local(): lax.psum_scatter(fc_grad, 'dp', scatter_dimension=0, tiled=True)  72.6 us
    reduce_scatter x1, waiting for transfers between devices, local(): lax.psum_scatter(qkv_grad, 'dp', scatter_dimension=0, tiled=True)  72.6 us
    psum x1, blocking collectives, local(): lax.psum((ln1_gain_grad, ln1_bias_grad, attn_out_bias_grad, ln2_gain_grad...  41.2 us
    all_gather x1, waiting for transfers between devices, local(): lax.all_gather(proj_weight.astype(jnp.bfloat16), 'dp', axis=1, tiled=True)  39 us
    all_gather x1, blocking collectives, local(): lax.all_gather(qkv_weight.astype(jnp.bfloat16), 'dp', axis=0, tiled=True)  38.6 us
    all_gather x2, waiting for transfers between devices, grad_rows(): return lax.all_gather(local_rows, 'tensor', axis=0, tiled=True)  37.6 us
    all_gather x1, blocking collectives, local(): lax.all_gather(attn_out_weight.astype(jnp.bfloat16), 'dp', axis=1, tiled=...  33 us
    unnamed x15, waiting for transfers between devices  30.8 us
  transfers between devices with their start and end apart: 23, of which 15 were waited for; matrix products, arithmetic and copies ran while one was open for 7% of the time, Pallas kernels for 0%

profile of v1, /device:TPU:0, one launch (start us, length us, event | category | flops | bytes accessed | tf_op | source)
XLA Modules:
  0.0 685.9 jit_solution(10482925746883633321)
XLA Ops:
  12.6 6.0 collective-permute-start
  21.1 2.8 collective-permute-start.3
  23.9 2.9 collective-permute-start.1
  30.4 3.2 collective-permute-done.2
  35.8 38.6 %all_gather.25 = bf16[768,3,192]{2,1,0:T(4,128)(2,1)S(1)} all-gather(bf16[96,3,192]{2,1,0:T(4,128)(2,1)S(1)} %copy.57), channel_id=1, replica_groups=mesh['dp'=8,'tensor'=4] {'dp'}, dimensions={0}, use_global_device_ids=true | all-gather | bytes 995328 | tf_op jit(solution)/shard_map/all_gather | solution.py:188
  75.4 33.0 %all_gather.26 = bf16[192,768]{0,1:T(8,128)(2,1)} all-gather(bf16[192,96]{0,1:T(8,128)(2,1)S(1)} %copy.60), channel_id=1, replica_groups=mesh['dp'=8,'tensor'=4] {'dp'}, dimensions={1}, use_global_device_ids=true | all-gather | bytes 331776 | tf_op jit(solution)/shard_map/all_gather | solution.py:189
  126.8 25.7 %reduce-scatter.11.cloned.1.call-done = bf16[256,768]{1,0:T(8,128)(2,1)} async-done(((bf16[1024,768]{1,0:T(8,128)(2,1)}), bf16[256,768]{1,0:T(8,128)(2,1)}) %reduce-scatter.11.cloned.1.call-update) | async-done | bytes 393232 | tf_op jit(solution)/shard_map/reduce_scatter | solution.py:218
  158.1 18.5 %all_to_all.27 = bf16[8,32,768]{2,1,0:T(8,128)(2,1)} all-to-all(bf16[8,32,768]{2,1,0:T(8,128)(2,1)} %get-tuple-element.131), channel_id=1, replica_groups=mesh['dp'=8,'tensor'=4] {'dp'}, dimensions={0} | all-to-all | bytes 786432 | tf_op jit(solution)/shard_map/all_to_all | solution.py:178
  177.2 13.9 %all-gather.9.cloned.1.call-done = bf16[1024,768]{1,0:T(8,128)(2,1)} async-done(((bf16[256,768]{1,0:T(8,128)(2,1)}), bf16[1024,768]{1,0:T(8,128)(2,1)}) %all-gather.9.cloned.1.call-update) | async-done | bytes 1572880 | tf_op jit(solution)/shard_map/all_gather | solution.py:223
  191.1 4.8 fusion.87
  195.9 39.0 %all-gather.13.cloned.1.call-done = bf16[768,768]{0,1:T(8,128)(2,1)} async-done(((bf16[768,96]{0,1:T(8,128)(2,1)}), bf16[768,768]{0,1:T(8,128)(2,1)}) %all-gather.13.cloned.1.call-update) | async-done | bytes 1179664 | tf_op jit(solution)/shard_map/all_gather | solution.py:191
  234.9 19.7 %all-gather.15.cloned.1.call-done = bf16[1024,768]{1,0:T(8,128)(2,1)} async-done(((bf16[256,768]{1,0:T(8,128)(2,1)}), bf16[1024,768]{1,0:T(8,128)(2,1)}) %all-gather.15.cloned.1.call-update) | async-done | bytes 1572880 | tf_op jit(solution)/shard_map/all_gather | solution.py:61
  254.6 6.9 %convert_reduce_fusion = (f32[768]{0:T(1024)}, bf16[1024,768]{1,0:T(8,128)(2,1)S(1)}) fusion(f32[1024,768]{1,0:T(8,128)} %fusion.87, f32[768]{0:T(1024)} %param.45, bf16[1024,768]{1,0:T(8,128)(2,1)} %all-gather.15.cloned.1.call-done, bf16[768,768]{0,1:T(8,128)(2,1)} %all-gather.13.cloned.1.call-done), kind=kOutput, calls=%fused_computation.23 | convolution fusion | flops 1229192448 | bytes 7477248 | tf_op jit(solution)/shard_map/dot_general | solution.py:32
  265.3 5.5 convolution_convert_fusion.2
  270.9 22.7 %reduce-scatter.15.cloned.1.call-done = bf16[256,768]{1,0:T(8,128)(2,1)} async-done(((bf16[1024,768]{1,0:T(8,128)(2,1)}), bf16[256,768]{1,0:T(8,128)(2,1)}) %reduce-scatter.15.cloned.1.call-update) | async-done | bytes 393232 | tf_op jit(solution)/shard_map/reduce_scatter | solution.py:65
  297.0 27.2 %reduce-scatter.13.cloned.1.call-done = bf16[256,768]{1,0:T(8,128)(2,1)} async-done(((bf16[1024,768]{1,0:T(8,128)(2,1)}), bf16[256,768]{1,0:T(8,128)(2,1)}) %reduce-scatter.13.cloned.1.call-update) | async-done | bytes 393232 | tf_op jit(solution)/shard_map/reduce_scatter | solution.py:226
  324.2 3.3 fusion.76
  330.8 18.0 %all-gather.17.cloned.1.call-done = bf16[1024,768]{1,0:T(8,128)(2,1)} async-done(((bf16[256,768]{1,0:T(8,128)(2,1)}), bf16[1024,768]{1,0:T(8,128)(2,1)}) %all-gather.17.cloned.1.call-update) | async-done | bytes 1572880 | tf_op jit(solution)/shard_map/all_gather | solution.py:61
  362.9 2.6 convolution_convert_fusion
  367.4 5.6 fusion.74
  373.3 5.1 fusion.88
  380.9 3.1 copy.64
  384.1 5.7 all-to-all-start
  389.8 4.0 reduce-scatter.17.cloned.1.call-done
  397.3 4.5 all-to-all-done
  401.9 3.6 all-to-all-start.2
  406.4 23.5 %all-reduce.3 = (f32[2,192]{1,0:T(2,128)}, f32[768]{0:T(1024)}) all-reduce(f32[2,192]{1,0:T(2,128)S(1)} %pad_maximum_fusion.4, f32[768]{0:T(1024)S(1)} %copy-done.52), channel_id=1, replica_groups=mesh['dp'=8,'tensor'=4] {'dp'}, use_global_device_ids=true, to_apply=%region_28.31 | all-reduce | flops 1152 | bytes 9216 | tf_op jit(solution)/shard_map/psum | solution.py:290
  429.9 30.6 %reduce-scatter.25.cloned.1.call-done = f32[96,192]{1,0:T(8,128)} async-done(((f32[768,192]{1,0:T(8,128)}), f32[96,192]{1,0:T(8,128)}) %reduce-scatter.25.cloned.1.call-update) | async-done | bytes 73744
  462.2 41.2 %all-reduce.2 = (f32[768]{0:T(1024)}, f32[768]{0:T(1024)}, f32[768]{0:T(1024)}, f32[768]{0:T(1024)}, f32[768]{0:T(1024)}, /*index=5*/f32[768]{0:T(1024)}) all-reduce(f32[768]{0:T(1024)S(1)} %get-tuple-element.84, f32[768]{0:T(1024)S(1)} %get-tuple-element.89, ...), channel_id=1, replica_groups=mesh['dp'=8,'tensor'=4] {'dp','tensor'}, use_global_device_ids=true, to_apply=%region_22.25 | all-reduce | flops 4608 | bytes 36864 | tf_op jit(solution)/shard_map/psum | solution.py:291
  505.0 28.4 %reduce-scatter.23.cloned.1.call-done = f32[768,96]{0,1:T(8,128)} async-done(((f32[768,768]{0,1:T(8,128)}), f32[768,96]{0,1:T(8,128)}) %reduce-scatter.23.cloned.1.call-update) | async-done | bytes 294928 | tf_op jit(solution)/shard_map/reduce_scatter | solution.py:287
  533.4 72.6 %reduce-scatter.21.cloned.1.call-done = f32[96,768]{1,0:T(8,128)} async-done(((f32[768,768]{1,0:T(8,128)}), f32[96,768]{1,0:T(8,128)}) %reduce-scatter.21.cloned.1.call-update) | async-done | bytes 294928 | tf_op jit(solution)/shard_map/reduce_scatter | solution.py:286
  606.0 72.6 %reduce-scatter.19.cloned.1.call-done = f32[96,3,192]{2,0,1:T(8,128)} async-done(((f32[768,3,192]{2,0,1:T(8,128)}), f32[96,3,192]{2,0,1:T(8,128)}) %reduce-scatter.19.cloned.1.call-update) | async-done | bytes 221200 | tf_op jit(solution)/shard_map/reduce_scatter | solution.py:284
  (251 shorter events, 74.5 us)
Async XLA Ops:
  8.0 102.7 %all-gather.7.cloned.1.call-start = ((), (), s32[]{:S(2)}) async-start(), calls=%async_computation.11 | async-start | bytes 1966080 | tf_op jit(solution)/shard_map/all_gather | solution.py:198
  12.6 11.3 %collective-permute-start = (bf16[32,768]{1,0:T(8,128)(2,1)S(1)}, bf16[32,768]{1,0:T(8,128)(2,1)S(1)}, u32[]{:S(2)}, u32[]{:S(2)}) collective-permute-start(bf16[32,768]{1,0:T(8,128)(2,1)S(1)} %get-tuple-element.120), channel_id=1, source_target_pairs={{0,28},{4,0},{8,4},{12,8},{16,12},{20,16},{24,20},{28,24},{1,29},{... | collective-permute-start | bytes 147464 | tf_op jit(solution)/shard_map/ppermute | solution.py:18
  18.6 15.0 %collective-permute-start.6 = (bf16[32,768]{1,0:T(8,128)(2,1)S(1)}, bf16[32,768]{1,0:T(8,128)(2,1)S(1)}, u32[]{:S(2)}, u32[]{:S(2)}) collective-permute-start(bf16[32,768]{1,0:T(8,128)(2,1)S(1)} %get-tuple-element.114), channel_id=1, source_target_pairs={{0,4},{4,8},{8,12},{12,16},{16,20},{20,24},{24,28},{28,0},{1,5},{5... | collective-permute-start | bytes 147464 | tf_op jit(solution)/shard_map/ppermute | solution.py:18
  18.6 15.0 %collective-permute-start.5 = (bf16[32,768]{1,0:T(8,128)(2,1)S(1)}, bf16[32,768]{1,0:T(8,128)(2,1)S(1)}, u32[]{:S(2)}, u32[]{:S(2)}) collective-permute-start(bf16[32,768]{1,0:T(8,128)(2,1)S(1)} %get-tuple-element.115), channel_id=1, source_target_pairs={{0,8},{4,12},{8,16},{12,20},{16,24},{20,28},{24,0},{28,4},{1,9},{5... | collective-permute-start | bytes 147464 | tf_op jit(solution)/shard_map/ppermute | solution.py:18
  18.6 15.0 %collective-permute-start.4 = (bf16[32,768]{1,0:T(8,128)(2,1)S(1)}, bf16[32,768]{1,0:T(8,128)(2,1)S(1)}, u32[]{:S(2)}, u32[]{:S(2)}) collective-permute-start(bf16[32,768]{1,0:T(8,128)(2,1)S(1)} %get-tuple-element.116), channel_id=1, source_target_pairs={{0,12},{4,16},{8,20},{12,24},{16,28},{20,0},{24,4},{28,8},{1,13},{... | collective-permute-start | bytes 147464 | tf_op jit(solution)/shard_map/ppermute | solution.py:18
  21.1 12.5 %collective-permute-start.3 = (bf16[32,768]{1,0:T(8,128)(2,1)S(1)}, bf16[32,768]{1,0:T(8,128)(2,1)S(1)}, u32[]{:S(2)}, u32[]{:S(2)}) collective-permute-start(bf16[32,768]{1,0:T(8,128)(2,1)S(1)} %get-tuple-element.117), channel_id=1, source_target_pairs={{0,16},{4,20},{8,24},{12,28},{16,0},{20,4},{24,8},{28,12},{1,17},{... | collective-permute-start | bytes 147464 | tf_op jit(solution)/shard_map/ppermute | solution.py:18
  23.9 4.7 collective-permute-start.1
  28.6 5.0 collective-permute-start.2
  34.1 41.2 %copy-start.42 = (f32[256]{0:T(256)}, f32[256]{0:T(256)S(1)}, u32[]{:S(2)}) copy-start(f32[256]{0:T(256)S(1)} %get-tuple-element.127) | copy-start | bytes 3076
  34.1 41.2 %copy-start.44 = (f32[256]{0:T(256)}, f32[256]{0:T(256)S(1)}, u32[]{:S(2)}) copy-start(f32[256]{0:T(256)S(1)} %get-tuple-element.128) | copy-start | bytes 3076
  35.1 73.3 %copy-start.54 = (f32[2,192]{1,0:T(2,128)S(1)}, f32[2,192]{1,0:T(2,128)}, u32[]{:S(2)}) copy-start(f32[2,192]{1,0:T(2,128)} %param.39) | copy-start | bytes 4612
  35.1 117.3 %reduce-scatter.11.cloned.1.call-start = ((), (), s32[]{:S(2)}) async-start(), calls=%async_computation.12 | async-start | bytes 1966080 | tf_op jit(solution)/shard_map/reduce_scatter | solution.py:218
  75.3 37.9 %copy-start.9 = (bf16[768,3,192]{0,2,1:T(8,128)(2,1)}, bf16[768,3,192]{0,2,1:T(8,128)(2,1)S(1)}, u32[]{:S(2)}) copy-start(bf16[768,3,192]{0,2,1:T(8,128)(2,1)S(1)} %copy.58) | copy-start | bytes 2654212
  122.4 32.0 %copy-start.37 = (f32[768]{0:T(1024)S(1)}, f32[768]{0:T(1024)}, u32[]{:S(2)}) copy-start(f32[768]{0:T(1024)} %param.42) | copy-start | bytes 9220
  125.0 52.2 %all-gather.11.cloned.1.call-start = ((), (), s32[]{:S(2)}) async-start(), calls=%async_computation.14 | async-start | bytes 1327104 | tf_op jit(solution)/shard_map/all_gather | solution.py:190
  126.7 64.3 %all-gather.9.cloned.1.call-start = ((), (), s32[]{:S(2)}) async-start(), calls=%async_computation.13 | async-start | bytes 1966080 | tf_op jit(solution)/shard_map/all_gather | solution.py:223
  156.4 78.6 %all-gather.13.cloned.1.call-start = ((), (), s32[]{:S(2)}) async-start(), calls=%async_computation.15 | async-start | bytes 1327104 | tf_op jit(solution)/shard_map/all_gather | solution.py:191
  158.1 96.5 %all-gather.15.cloned.1.call-start = ((), (), s32[]{:S(2)}) async-start(), calls=%async_computation.17 | async-start | bytes 1966080 | tf_op jit(solution)/shard_map/all_gather | solution.py:61
  176.7 116.9 %reduce-scatter.15.cloned.1.call-start = ((), (), s32[]{:S(2)}) async-start(), calls=%async_computation.18 | async-start | bytes 1966080 | tf_op jit(solution)/shard_map/reduce_scatter | solution.py:65
  265.3 58.9 %reduce-scatter.13.cloned.1.call-start = ((), (), s32[]{:S(2)}) async-start(), calls=%async_computation.16 | async-start | bytes 1966080 | tf_op jit(solution)/shard_map/reduce_scatter | solution.py:226
  270.9 77.9 %all-gather.17.cloned.1.call-start = ((), (), s32[]{:S(2)}) async-start(), calls=%async_computation.19 | async-start | bytes 1966080 | tf_op jit(solution)/shard_map/all_gather | solution.py:61
  329.2 64.6 %reduce-scatter.17.cloned.1.call-start = ((), (), s32[]{:S(2)}) async-start(), calls=%async_computation.20 | async-start | bytes 1966080 | tf_op jit(solution)/shard_map/reduce_scatter | solution.py:65
  365.6 95.0 %reduce-scatter.25.cloned.1.call-start = ((), (), s32[]{:S(2)}) async-start(), calls=%async_computation.24 | async-start | bytes 884736
  367.3 166.1 %reduce-scatter.23.cloned.1.call-start = ((), (), s32[]{:S(2)}) async-start(), calls=%async_computation.23 | async-start | bytes 2654208 | tf_op jit(solution)/shard_map/reduce_scatter | solution.py:287
  373.0 232.9 %reduce-scatter.21.cloned.1.call-start = ((), (), s32[]{:S(2)}) async-start(), calls=%async_computation.22 | async-start | bytes 2654208 | tf_op jit(solution)/shard_map/reduce_scatter | solution.py:286
  378.4 300.1 %reduce-scatter.19.cloned.1.call-start = ((), (), s32[]{:S(2)}) async-start(), calls=%async_computation.21 | async-start | bytes 2654208 | tf_op jit(solution)/shard_map/reduce_scatter | solution.py:284
  384.0 78.1 %copy-start.48 = (f32[768]{0:T(1024)S(1)}, f32[768]{0:T(1024)}, u32[]{:S(2)}) copy-start(f32[768]{0:T(1024)} %get-tuple-element.80) | copy-start | bytes 9220
  384.0 78.1 %copy-start.49 = (f32[768]{0:T(1024)S(1)}, f32[768]{0:T(1024)}, u32[]{:S(2)}) copy-start(f32[768]{0:T(1024)} %get-tuple-element.88) | copy-start | bytes 9220
  384.0 78.1 %copy-start.50 = (f32[768]{0:T(1024)S(1)}, f32[768]{0:T(1024)}, u32[]{:S(2)}) copy-start(f32[768]{0:T(1024)} %get-tuple-element.104) | copy-start | bytes 9220
  384.1 17.8 %all-to-all-start = ((bf16[8,32,768]{2,1,0:T(8,128)(2,1)}), bf16[8,32,768]{2,1,0:T(8,128)(2,1)S(1)}, u32[]{:S(2)}, u32[]{:S(2)}) async-start(bf16[8,32,768]{2,1,0:T(8,128)(2,1)} %bitcast.15), calls=%async_computation.2 | async-start | bytes 786432 | tf_op jit(solution)/shard_map/all_to_all | solution.py:274
  395.2 283.4 %copy-start.1 = (bf16[256,768]{1,0:T(8,128)(2,1)S(1)}, bf16[256,768]{1,0:T(8,128)(2,1)}, u32[]{:S(2)}) copy-start(bf16[256,768]{1,0:T(8,128)(2,1)} %param.33) | copy-start | bytes 1179652
  401.9 101.5 %all-to-all-start.2 = ((bf16[8,32,768]{2,1,0:T(8,128)(2,1)}), bf16[8,32,768]{2,1,0:T(8,128)(2,1)S(1)}, u32[]{:S(2)}, u32[]{:S(2)}) async-start(bf16[8,32,768]{2,1,0:T(8,128)(2,1)} %bitcast.30), calls=%async_computation.6 | async-start | bytes 786432 | tf_op jit(solution)/shard_map/all_to_all | solution.py:275
  (52 other events, 370.2 us)
Sparse Core Ops, SparseCore 0:
  35.3 22.3 all-gather.6
  125.1 27.2 reduce-scatter.10
  265.4 28.1 reduce-scatter.14
  296.0 28.1 reduce-scatter.12
Sparse Core Ops, SparseCore 1:
  128.5 41.5 all-gather.10
  172.1 18.9 all-gather.8
  193.4 41.5 all-gather.12
  236.6 18.0 all-gather.14
  329.2 19.5 all-gather.16
  365.6 28.0 reduce-scatter.16
  396.9 63.6 reduce-scatter.24
  464.9 68.5 reduce-scatter.22
  537.8 68.2 reduce-scatter.20
  610.5 68.0 reduce-scatter.18
